TPU v7x, 256 devices: a whole 4x4x8 slice. The times are simulated.
256 devices in a mesh: gx: 4 (over x), gy: 8 (over y, core), gz: 8 (over z).
Axes of the slice: x: 4, y: 4, z: 8, core: 2. Of those that a mesh axis runs over, the one named last changes fastest.
Arguments:
- volume: bfloat16 [32, 64, 32, 1024], P(None, 'gz', 'gx', 'gy'), may hold values from -6 to 6
- cotangent: bfloat16 [32, 64, 32, 1024], P(None, 'gz', 'gx', 'gy'), may hold values from -6 to 6
- weight_one: bfloat16 [27, 32, 32], replicated, may hold values from -0.21875 to 0.21875
- weight_two: bfloat16 [27, 64, 32], replicated, may hold values from -0.21875 to 0.21875
- weight_three: bfloat16 [27, 256, 64], replicated, may hold values from -0.15625 to 0.15625
- weight_four: bfloat16 [32, 256], replicated, may hold values from -0.375 to 0.375
Outputs:
- output: bfloat16 [32, 64, 32, 1024], P(None, 'gz', 'gx', 'gy')
- grad_volume: bfloat16 [32, 64, 32, 1024], P(None, 'gz', 'gx', 'gy')
- grad_one: float32 [27, 32, 32], replicated
- grad_two: float32 [27, 64, 32], replicated
- grad_three: float32 [27, 256, 64], replicated
- grad_four: float32 [32, 256], replicated
All inputs are finite; a program needn't handle non-finite values.
Results may differ from a plain program's by a relative error of at most 0.027.
Values may be sent and summed in bfloat16 or wider, within the bound.
A program may use at most 128 MiB of HBM per device.

v0:
```python
import functools
import itertools
import math

import jax
import jax.numpy as jnp
from jax import lax
from jax.experimental import pallas as pl
from jax.experimental.pallas import tpu as pltpu
from jax.sharding import PartitionSpec as P

MESH = pl.DeviceIdType.MESH
BF = jnp.bfloat16
F32 = jnp.float32
INV8 = 1.0 / math.sqrt(8.0)
STEPS = sorted(
    (d for d in itertools.product((-1, 0, 1), repeat=3) if d != (0, 0, 0)),
    key=lambda d: -sum(map(abs, d)),
)

NN = ((1,), (0,))
NT = ((1,), (1,))
TN = ((0,), (0,))


def dot(a, b, dims=NN):
    return lax.dot_general(a, b, (dims, ((), ())), preferred_element_type=F32)


def rows_cols(shape):
    return (
        lax.broadcasted_iota(jnp.int32, shape, 0),
        lax.broadcasted_iota(jnp.int32, shape, 1),
    )


def hot(cond):
    return jnp.where(cond, 1.0, 0.0).astype(BF)


def roll(a, shift):
    return pltpu.roll(a, shift % a.shape[1], 1)


def silu_slope(pre):
    sig = 0.5 * (1.0 + jnp.tanh(0.5 * pre))
    act = pre * sig
    return act, sig + act * (1.0 - sig)


def split(a):
    high = a.astype(BF)
    return high, (a - high.astype(F32)).astype(BF)


class Place:
    def __init__(self, sizes):
        self.size = dict(zip(("x", "y", "z"), sizes))
        self.at = {
            "x": lax.axis_index("gx"),
            "y": lax.axis_index("gy"),
            "z": lax.axis_index("gz"),
        }

    def near(self, axis, step):
        size = self.size[axis]
        return lax.rem(self.at[axis] + (step + size), size)

    def device(self, dz, dx, dy):
        return (self.near("x", dx), self.near("y", dy), self.near("z", dz))

    def inside(self, axis, step):
        if step == 0:
            return None
        if step < 0:
            return self.at[axis] > 0
        return self.at[axis] < self.size[axis] - 1


class Halo:
    def __init__(self, place, pad, face, got, send, recv, nz, nx, ch, ylen):
        self.place, self.pad, self.face, self.got = place, pad, face, got
        self.send, self.recv = send, recv
        self.nz, self.nx, self.ch, self.ylen = nz, nx, ch, ylen

    def put(self, z, value):
        self.pad[z + 1, self.ch : self.ch * (self.nx + 1), :] = value

    def start(self):
        nz, nx, ch = self.nz, self.nx, self.ch
        r, c = rows_cols((32, nz * 128))
        edge = jnp.where(r >= 16, self.ylen - 1, 0)
        pick = hot(((r & 15) == (c >> 7)) & ((c & 127) == edge))
        own = jnp.concatenate(
            [self.pad[z + 1, ch : ch * (nx + 1), :] for z in range(nz)], axis=1
        )
        both = dot(pick, own, NT).astype(BF)
        self.face[0] = both[:16]
        self.face[1] = both[16:]
        self.copies = []
        for i, (dz, dx, dy) in enumerate(STEPS):
            if dy == 0:
                zs = {-1: (1, 1), 0: (1, nz), 1: (nz, 1)}[dz]
                xs = {-1: (ch, ch), 0: (ch, nx * ch), 1: (nx * ch, ch)}[dx]
                zd = {-1: nz + 1, 0: 1, 1: 0}[dz]
                xd = {-1: (nx + 1) * ch, 0: ch, 1: 0}[dx]
                src = self.pad.at[pl.ds(zs[0], zs[1]), pl.ds(xs[0], xs[1])]
                dst = self.pad.at[pl.ds(zd, zs[1]), pl.ds(xd, xs[1])]
            else:
                side = 0 if dy == 1 else 1
                src = self.face.at[1 - side]
                dst = self.got.at[1 - dx, side, 1 - dz]
            copy = pltpu.make_async_remote_copy(
                src_ref=src,
                dst_ref=dst,
                send_sem=self.send.at[i],
                recv_sem=self.recv.at[i],
                device_id=self.place.device(dz, dx, dy),
                device_id_type=MESH,
            )
            copy.start()
            self.copies.append(copy)

    def arrive(self):
        for copy in self.copies:
            copy.wait_recv()
        nz, nx, ch = self.nz, self.nx, self.ch
        at, size = self.place.at, self.place.size
        plane = jnp.zeros(self.pad.shape[1:], BF)
        column = jnp.zeros((nz + 2, ch, 128), BF)

        @pl.when(at["z"] == 0)
        def _():
            self.pad[0] = plane

        @pl.when(at["z"] == size["z"] - 1)
        def _():
            self.pad[nz + 1] = plane

        @pl.when(at["x"] == 0)
        def _():
            self.pad[:, 0:ch, :] = column

        @pl.when(at["x"] == size["x"] - 1)
        def _():
            self.pad[:, (nx + 1) * ch :, :] = column

    def columns(self):
        nz, nx, ch = self.nz, self.nx, self.ch
        at, size = self.place.at, self.place.size
        r, c = rows_cols((96, 128))
        group, z = r >> 4, r & 15
        side = jnp.where(group >= 3, 1, 0)
        dz = group - 3 * side
        zp = c & 15
        first, last = (
            jnp.where(at["z"] > 0, 0, -1),
            jnp.where(at["z"] < size["z"] - 1, nz + 1, -1),
        )
        low, high = (
            jnp.where(at["y"] > 0, 0, -1),
            jnp.where(at["y"] < size["y"] - 1, 1, -1),
        )
        mid = (dz == 1) & (z < nz) & (zp == z + 1)
        below = (dz == 0) & (z == nz - 1) & (zp == first)
        above = (dz == 2) & (z == 0) & (zp == last)
        lane = (side == (c >> 4)) & ((side == low) | (side == high))
        pick = hot((mid | below | above) & lane)
        parts = []
        for dx in range(3):
            wide = slice(0, nx * ch)
            if dx == 0:
                wide = slice((nx - 1) * ch, nx * ch)
            if dx == 2:
                wide = slice(0, ch)
            src = self.got[dx].reshape(96, nx * ch)[:, wide]
            part = dot(src, pick, TN)
            if dx != 1:
                part = jnp.where(self.place.inside("x", dx - 1), part, 0.0)
            parts.append(part.astype(BF))
        return jnp.concatenate(parts, axis=0)

    def shifted(self):
        cols = self.columns()
        lane = rows_cols(cols.shape)[1]
        for zp in range(self.nz + 2):
            base = self.pad[zp]
            low = jnp.where(lane == 0, roll(cols, -zp), roll(base, 1))
            end = self.ylen - 1
            high = jnp.where(lane == end, roll(cols, end - 16 - zp), roll(base, -1))
            yield zp, (low, base, high)

    def finish(self):
        for copy in self.copies:
            copy.wait_send()


def fill_fine(halo, u):
    rows = (halo.nx + 2) * halo.ch
    for zp, parts in halo.shifted():
        for ky, part in enumerate(parts):
            if zp <= 5:
                u[zp, ky * rows : (ky + 1) * rows, 0:128] = part
            if zp >= 4:
                u[zp - 4, ky * rows : (ky + 1) * rows, 128:256] = part


def fill_half(halo, u):
    before = None
    for zp, parts in halo.shifted():
        if before is not None:
            j = zp - 1
            for ky in range(3):
                lane = rows_cols(parts[ky].shape)[1]
                both = jnp.where(lane < 64, before[ky], roll(parts[ky], 64))
                if j <= 2:
                    u[j * 3 + ky, :, 0:128] = both
                if j >= 2:
                    u[(j - 2) * 3 + ky, :, 128:256] = both
        before = parts


def put_half(halo, value):
    lane = rows_cols((value.shape[0], 128))[1]
    for z in range(4):
        half = value[:, 128 * (z // 2) : 128 * (z // 2) + 128]
        if z % 2:
            half = roll(half, 64)
        halo.put(z, jnp.where(lane < 64, half, jnp.zeros_like(half)))


def toeplitz(dst, blocks, nx, rows, width):
    dst[...] = jnp.zeros(dst.shape, BF)
    for kz, ky in itertools.product(range(3), range(3)):
        band = jnp.concatenate([blocks(kz, kx, ky) for kx in range(3)], axis=1)
        base = (kz * 3 + ky) * (nx + 2) * width
        for x in range(nx):
            dst[rows * x : rows * (x + 1), base + width * x : base + width * (x + 3)] = band


def coarse_start(place, box, send, recv):
    copies = []
    for i, (dz, dx, dy) in enumerate(STEPS):
        copy = pltpu.make_async_remote_copy(
            src_ref=box.at[1, 1, 1],
            dst_ref=box.at[1 - dz, 1 - dx, 1 - dy],
            send_sem=send.at[i],
            recv_sem=recv.at[i],
            device_id=place.device(dz, dx, dy),
            device_id_type=MESH,
        )
        copy.start()
        copies.append(copy)
    return copies


def coarse_shifts(place, box):
    wide = []
    for dz, dx in itertools.product((-1, 0, 1), (-1, 0, 1)):
        rows = []
        for dy in (-1, 0, 1):
            block = box[dz + 1, dx + 1, dy + 1]
            for axis, step in (("z", dz), ("x", dx), ("y", dy)):
                if step:
                    block = jnp.where(place.inside(axis, step), block, jnp.zeros_like(block))
            rows.append(block)
        wide.append(jnp.concatenate(rows, axis=0))
    wide = jnp.concatenate(wide, axis=1)
    r, c = rows_cols((48, 48))
    pick = hot(c == (r & 15) + (r >> 4) + 15)
    width = box.shape[-1]
    return dot(pick, wide).astype(BF), wide[8:40, 4 * width : 5 * width]


class Group:
    def __init__(self, place, kind, send, recv):
        self.place, self.kind, self.send, self.recv = place, kind, send, recv
        size = place.size
        self.count = {
            "plane": size["x"] * size["z"],
            "sheet": size["x"] * size["y"],
            "line": size["y"],
            "depth": size["z"],
            "chips": size["y"] // 2,
            "cores": 2,
        }[kind]

    def member(self, q):
        at, size = self.place.at, self.place.size
        if self.kind == "plane":
            x = lax.rem(at["x"] + q // size["z"], size["x"])
            z = lax.rem(at["z"] + lax.rem(q, size["z"]), size["z"])
            return (x, at["y"], z), x * size["z"] + z
        if self.kind == "sheet":
            x = lax.rem(at["x"] + q // size["y"], size["x"])
            y = lax.rem(at["y"] + lax.rem(q, size["y"]), size["y"])
            return (x, y, at["z"]), x * size["y"] + y
        if self.kind == "depth":
            z = lax.rem(at["z"] + q, size["z"])
            return (at["x"], at["y"], z), z
        if self.kind == "line":
            y = lax.rem(at["y"] + q, size["y"])
            return (at["x"], y, at["z"]), y
        if self.kind == "chips":
            y = lax.rem(at["y"] + 2 * q, size["y"])
            return (at["x"], y, at["z"]), y // 2
        y = at["y"] + 1 - 2 * lax.rem(at["y"], 2)
        return (at["x"], y, at["z"]), lax.rem(y, 2)

    def start(self, src, dst):
        def one(q, carry):
            device, index = self.member(q)
            pltpu.make_async_remote_copy(
                src_ref=src(index),
                dst_ref=dst,
                send_sem=self.send,
                recv_sem=self.recv,
                device_id=device,
                device_id_type=MESH,
            ).start()
            return carry

        lax.fori_loop(1, self.count, one, 0)

    def _all(self, slots):
        ref = slots.at[pl.ds(0, self.count - 1)]
        return pltpu.make_async_remote_copy(
            src_ref=ref,
            dst_ref=ref,
            send_sem=self.send,
            recv_sem=self.recv,
            device_id=self.member(1)[0],
            device_id_type=MESH,
        )

    def arrive(self, slots):
        if self.count > 1:
            self._all(slots).wait_recv()

    def finish(self, slots):
        if self.count > 1:
            self._all(slots).wait_send()


class Total:
    def __init__(self, place, mine, landed, line, done, send, recv):
        self.mine, self.landed, self.line, self.done = mine, landed, line, done
        self.at = place.at
        self.me = place.at["x"] * place.size["y"] + place.at["y"]
        self.one = Group(place, "sheet", send.at[0], recv.at[0])
        self.two = Group(place, "depth", send.at[1], recv.at[1])
        self.three = Group(place, "sheet", send.at[2], recv.at[2])

    def scatter(self):
        self.one.start(lambda index: self.mine.at[index], self.landed.at[self.me])
        self.landed[self.me] = self.mine[self.me]

    def cross(self):
        self.one.arrive(self.landed)
        self.line[self.at["z"]] = jnp.sum(self.landed[...], axis=0)
        own = self.line.at[self.at["z"]]
        self.two.start(lambda index: own, own)

    def gather(self, scale):
        self.two.arrive(self.line)
        total = jnp.sum(self.line[...], axis=0) * scale
        self.done[self.me] = total.astype(self.done.dtype)
        own = self.done.at[self.me]
        self.three.start(lambda index: own, own)

    def arrive(self):
        self.three.arrive(self.done)

    def finish(self):
        self.one.finish(self.landed)
        self.two.finish(self.line)
        self.three.finish(self.done)


def kernel(
    sizes, scales, vol_in, cot_in, w1_in, w2_in, w3_in, w4_in,
    out, gvol, d1, d2, d3,
    v_pad, v_face, v_got, q_pad, q_face, q_got,
    h_pad, h_face, h_got, g_pad, g_face, g_got,
    u1, ug, u2, uh, t1, tt1, t2, tt2,
    sl1, act1, cot1, g1, box_in, box_gp, send, recv,
    note, seen, near_y, tap_sum, tap_line, tap_all,
    m1, l1, y1, f1, m2, l2, y2, f2, gsend, grecv,
    vol, cot, w1, w2, w3, w4, out_rows, gvol_rows, local,
):
    place = Place(sizes)
    seen[...] = jnp.zeros(seen.shape, BF)
    barrier = pltpu.get_barrier_semaphore()
    partners = [place.device(*s) for s in STEPS if s[0] != 0 and s[2] != 0]
    for device in partners:
        pl.semaphore_signal(barrier, inc=1, device_id=device, device_id_type=MESH)
    sums = [
        Group(place, kind, gsend.at[i], grecv.at[i])
        for i, kind in enumerate(("plane", "line", "plane", "chips", "cores"))
    ]
    gather, across, plane, chips, cores = sums
    total = len(partners)
    for kind in ("plane", "sheet"):
        group = Group(place, kind, None, None)

        def greet(q, carry, group=group):
            device = group.member(q)[0]
            pl.semaphore_signal(barrier, inc=1, device_id=device, device_id_type=MESH)
            return carry

        lax.fori_loop(1, group.count, greet, 0)
        total += group.count - 1
    loads = [
        pltpu.make_async_copy(src, dst, local.at[i])
        for i, (src, dst) in enumerate(
            (
                (vol_in, vol), (cot_in, cot), (w1_in, w1),
                (w2_in, w2), (w3_in, w3), (w4_in, w4),
            )
        )
    ]
    for load in loads:
        load.start()
    stores = []

    def store(src, dst):
        copy = pltpu.make_async_copy(src, dst, local.at[len(loads) + len(stores)])
        copy.start()
        stores.append(copy)

    ix, iy, iz = place.at["x"], place.at["y"], place.at["z"]
    nx, nz = place.size["x"], place.size["z"]
    me = ix * nz + iz
    m1[27:32] = jnp.zeros((5, 8, 128), F32)
    m2[27:32] = jnp.zeros((5, 16, 128), F32)
    r, c = rows_cols((256, 256))
    perm = hot(((r & 31) == (c >> 3)) & ((r >> 5) == (c & 7)))

    def two(ref, zz):
        return jnp.concatenate(
            [ref[:, zz].reshape(256, 128), ref[:, zz + 4].reshape(256, 128)], axis=1
        )

    hv = Halo(place, v_pad, v_face, v_got, send.at[0], recv.at[0], 8, 8, 32, 128)
    hq = Halo(place, q_pad, q_face, q_got, send.at[1], recv.at[1], 4, 4, 32, 64)
    hh = Halo(place, h_pad, h_face, h_got, send.at[2], recv.at[2], 4, 4, 64, 64)
    hg = Halo(place, g_pad, g_face, g_got, send.at[3], recv.at[3], 8, 8, 32, 128)
    sum1 = Total(place, m1, l1, y1, f1, gsend.at[pl.ds(5, 3)], grecv.at[pl.ds(5, 3)])
    sum2 = Total(place, m2, l2, y2, f2, gsend.at[pl.ds(8, 3)], grecv.at[pl.ds(8, 3)])
    loads[0].wait()
    for zz in range(4):
        rows = dot(perm, two(vol, zz)).astype(BF)
        hv.put(zz, rows[:, :128])
        hv.put(zz + 4, rows[:, 128:])
    pl.semaphore_wait(barrier, total)
    hv.start()
    for load in loads[1:]:
        load.wait()

    for zz in range(4):
        cot1[zz] = dot(perm, two(cot, zz)).astype(BF)
    r, c = rows_cols((32, 32))
    eye = hot(r == c)
    toeplitz(t1, lambda kz, kx, ky: w1[kz * 9 + kx * 3 + ky], 8, 32, 32)
    flat1 = dot(eye, w1[...].reshape(864, 32), NT).astype(BF)
    r, c = rows_cols((64, 64))
    flat2 = dot(hot(r == c), w2[...].reshape(864, 64), NT).astype(BF)

    def back_tap(kz, kx, ky):
        return (2 - kz) * 9 + (2 - kx) * 3 + (2 - ky)

    def turned(kz, kx, ky):
        k = back_tap(kz, kx, ky)
        return flat1[:, k * 32 : (k + 1) * 32]

    def straight(kz, kx, ky):
        k = kz * 9 + kx * 3 + ky
        return flat2[:, k * 32 : (k + 1) * 32]

    toeplitz(t2, straight, 4, 64, 32)
    toeplitz(tt1, turned, 8, 32, 32)
    toeplitz(tt2, lambda *k: w2[back_tap(*k)], 4, 32, 64)
    cg = jnp.sum(cot[...].astype(F32), axis=(1, 2))
    cg = cg + roll(cg, -1)
    cg = cg + roll(cg, -2)
    cg = (cg + roll(cg, -4)).astype(BF)

    hv.arrive()
    fill_fine(hv, u1)
    for zz in range(4):
        pre = dot(t1[...], u1[zz : zz + 3].reshape(2880, 256))
        act, slope = silu_slope(pre)
        act1[zz] = act.astype(BF)
        sl1[zz] = slope
    r, c = rows_cols((512, 256))
    z2 = 2 * ((r >> 7) & 1) + (r >> 8)
    pick = hot(((c >> 6) == z2) & ((r & 127) == 2 * (c & 63)))
    pooled = []
    for a, b in ((0, 1), (2, 3)):
        s = act1[a].astype(F32) + act1[b].astype(F32)
        s = jnp.sum(s.reshape(4, 2, 32, 256), axis=1).reshape(128, 256)
        s = s + roll(s, -1)
        pooled.append((s * INV8).astype(BF))
    q1 = dot(jnp.concatenate(pooled, axis=1), pick).astype(BF)
    put_half(hq, q1)
    hq.start()

    hq.arrive()
    fill_half(hq, u2)
    pre2 = dot(t2[...], u2[...].reshape(1728, 256))
    act2, slope2 = silu_slope(pre2)
    s = jnp.sum(act2.astype(BF).astype(F32).reshape(4, 64, 256), axis=0)
    s = s[:, :128] + s[:, 128:]
    s = s + roll(s, 64)
    s = s + roll(s, -1)
    s = s + roll(s, -2)
    cin = (s * 0.125).astype(BF)
    zero = jnp.zeros((64, 128), BF)
    r, c = rows_cols((16, 128))
    own = dot(hot(c == 4 * r), jnp.concatenate([cin, zero], axis=0), NT)
    own += dot(hot(c == 8 * r), jnp.concatenate([zero, cg, zero[:32]], axis=0), NT)
    own = own.astype(BF)
    box_in[1, 1, 1] = own
    first = coarse_start(place, box_in, send.at[4], recv.at[4])
    for copy in first:
        copy.wait_recv()
    near, own = coarse_shifts(place, box_in)
    note[...] = own

    def tap(kz, kx, ky, width, valid):
        base = (kz * 3 + kx) * width
        return near[16 * ky : 16 * (ky + 1), base : base + valid]

    taps = list(itertools.product(range(3), range(3), range(3)))
    x3 = jnp.concatenate([tap(*k, 128, 64) for k in taps], axis=1)
    pre3 = dot(x3, w3[...].reshape(1728, 256))
    act3, slope3 = silu_slope(pre3)
    act3 = act3.astype(BF)
    cgt = own[8:24, 64:96]
    gp3 = (dot(cgt, w4[...]) * slope3).astype(BF)
    box_gp[1, 1, 1] = gp3
    second = coarse_start(place, box_gp, send.at[5], recv.at[5])
    gather.start(lambda index: note, seen.at[(iz + 1) * (nx + 2) + ix + 1])
    seen[(iz + 1) * (nx + 2) + ix + 1] = own
    co = dot(w4[...], act3, NT).astype(BF)
    part4 = dot(cgt, act3, TN)
    for i in range(4):
        half, col = i % 2, 128 * (i // 2)
        m2[27 + i] = part4[16 * half : 16 * half + 16, col : col + 128]
    r, c = rows_cols((16, 128))
    co = dot(co, hot(r == (c >> 3)))
    co = jnp.concatenate([jnp.concatenate([co] * 8, axis=0)] * 2, axis=1)
    for zz in range(4):
        out_rows[zz] = (act1[zz].astype(F32) + co).astype(BF)
    store(out_rows, out)
    for copy in second:
        copy.wait_recv()
    near = coarse_shifts(place, box_gp)[0]
    gc = sum(
        dot(w3[kz * 9 + kx * 3 + ky], tap(2 - kz, 2 - kx, 2 - ky, 256, 256), NT)
        for kz, kx, ky in taps
    )
    r, c = rows_cols((16, 256))
    pick = hot(r == ((c & 63) >> 2))
    up = sum(dot(part, pick) for part in split(gc)) * 0.125
    gp2 = (jnp.concatenate([up] * 4, axis=0) * slope2).astype(BF)
    put_half(hh, gp2)
    hh.start()
    lane = rows_cols((16, 128))[1]
    for kz in range(3):
        g = dot(u2[3 * kz : 3 * kz + 3].reshape(576, 256), gp2, NT)
        for ky, kx in itertools.product(range(3), range(3)):
            cut = [
                g[ky * 192 + 32 * (x + kx) :][:32, 128 * (x // 2) : 128 * (x // 2) + 128]
                for x in range(4)
            ]
            even, odd = cut[0] + cut[2], cut[1] + cut[3]
            low = (even + roll(odd, 64))[:16]
            high = (roll(even, 64) + odd)[16:]
            m2[kz * 9 + kx * 3 + ky] = jnp.where(lane < 64, low, high)
    sum2.scatter()
    gather.arrive(seen)
    for ky in range(3):
        near_y[ky] = seen[:, 7 + ky : 23 + ky, :]
    lane = rows_cols((16, 128))[1]
    pair = jnp.where(lane < 64, near_y[0], pltpu.roll(near_y[1], 64, 2))
    both = jnp.concatenate([pair, near_y[2]], axis=2)
    both = both.reshape(nz + 2, nx + 2, 16, 256)
    pre = sum(
        dot(
            both[kz : kz + nz, kx : kx + nx].reshape(nz * nx * 16, 256)[:, :192],
            w3[kz * 9 + kx * 3 : kz * 9 + kx * 3 + 3].reshape(192, 256),
        )
        for kz, kx in itertools.product(range(3), range(3))
    )
    slope = silu_slope(pre)[1]
    mid = near_y[1].reshape(nz + 2, nx + 2, 16, 128)[1 : nz + 1, 1 : nx + 1]
    mid = mid.reshape(nz * nx * 16, 128)[:, 64:96]
    gp = (dot(mid, w4[...]) * slope).astype(BF)
    k = lax.rem(me, 27)
    kz, kx, ky = k // 9, lax.rem(k // 3, 3), lax.rem(k, 3)
    rows = jnp.concatenate(
        [
            near_y[ky, pl.ds((z + kz) * (nx + 2) + kx, nx)].reshape(nx * 16, 128)
            for z in range(nz)
        ],
        axis=0,
    )
    tap_sum[...] = dot(rows, gp, TN)[:64].reshape(8, 8, 256)
    across.start(lambda index: tap_sum.at[index], tap_line.at[iy])
    tap_line[iy] = tap_sum[iy]
    hh.arrive()
    across.arrive(tap_line)
    s = jnp.sum(tap_line[...], axis=0) * scales[2]
    tap_all[iy, me] = jnp.concatenate([s[:, :128], s[:, 128:]], axis=0).astype(BF)
    own_tap = tap_all.at[iy, me]
    plane.start(lambda index: own_tap, own_tap)
    sum2.cross()
    fill_half(hh, uh)
    gpool = dot(tt2[...], uh[...].reshape(3456, 256))
    r, c = rows_cols((256, 256))
    parts = split(gpool)
    for h in range(2):
        pick = hot(((r >> 6) == 2 * (c >> 7) + h) & ((r & 63) == ((c & 127) >> 1)))
        up = sum(dot(part, pick) for part in parts) * INV8
        up = jnp.concatenate(
            [up[32 * (x // 2) : 32 * (x // 2) + 32] for x in range(8)], axis=0
        )
        for zz in (2 * h, 2 * h + 1):
            gp1 = ((cot1[zz].astype(F32) + up) * sl1[zz]).astype(BF)
            hg.put(zz, gp1[:, :128])
            hg.put(zz + 4, gp1[:, 128:])
            g1[:, 256 * zz : 256 * zz + 256] = gp1
    for kz in range(3):
        uc = jnp.concatenate([u1[kz + zz] for zz in range(4)], axis=1)
        g = dot(g1[...], uc, NT)
        for ky in range(3):
            band = sum(
                g[32 * x : 32 * x + 32, ky * 320 + 32 * x : ky * 320 + 32 * x + 96]
                for x in range(8)
            )
            for kx in range(3):
                m1[kz * 9 + kx * 3 + ky] = jnp.concatenate(
                    [band[8 * i : 8 * i + 8, 32 * kx : 32 * kx + 32] for i in range(4)],
                    axis=1,
                )
    sum1.scatter()
    hg.start()
    plane.arrive(tap_all.at[iy])
    own_range = tap_all.at[iy]
    chips.start(lambda index: own_range, own_range)
    sum1.cross()
    sum2.gather(scales[1])
    hg.arrive()
    fill_fine(hg, ug)
    sum1.gather(scales[0])
    for zz in range(4):
        rows = dot(tt1[...], ug[zz : zz + 3].reshape(2880, 256))
        gvol_rows[zz] = rows.astype(BF)
    store(gvol_rows, gvol)
    chips.arrive(tap_all)
    core = lax.rem(iy, 2)

    def to_core(c, carry):
        own = tap_all.at[2 * c + core]
        pltpu.make_async_remote_copy(
            src_ref=own,
            dst_ref=own,
            send_sem=cores.send,
            recv_sem=cores.recv,
            device_id=cores.member(1)[0],
            device_id_type=MESH,
        ).start()
        return carry

    lax.fori_loop(0, chips.count, to_core, 0)
    sum2.arrive()
    store(f2, d2)
    sum1.arrive()
    store(f1, d1)
    rest = tap_all.at[pl.ds(0, chips.count)]
    rest = pltpu.make_async_remote_copy(
        src_ref=rest,
        dst_ref=rest,
        send_sem=cores.send,
        recv_sem=cores.recv,
        device_id=cores.member(1)[0],
        device_id_type=MESH,
    )
    rest.wait_recv()
    store(tap_all, d3)
    rest.wait_send()
    for halo in (hv, hq, hh, hg):
        halo.finish()
    for copy in first + second:
        copy.wait_send()
    gather.finish(seen)
    across.finish(tap_line)
    plane.finish(tap_all.at[iy])
    chips.finish(tap_all)
    sum1.finish()
    sum2.finish()
    for copy in stores:
        copy.wait()


def last_kernel(
    scale, out_rows, gvol_rows, f1, f2, tap_all,
    out, gvol, d1, d2, d3, d4,
    out_v, gvol_v, v1, v2, v3, sems,
):
    r, c = rows_cols((256, 256))
    back = hot(((c & 31) == (r >> 3)) & ((c >> 5) == (r & 7)))
    copies = []

    def store(src, dst):
        copy = pltpu.make_async_copy(src, dst, sems.at[len(copies)])
        copy.start()
        copies.append(copy)

    for j in range(tap_all.shape[0]):
        for k in range(27):
            block = tap_all[j, k].astype(F32)
            v3[k, 8 * j : 8 * j + 8, :] = jnp.concatenate([block[:8], block[8:]], axis=1)
    store(v3, d3)
    for src, mid, dst in ((out_rows, out_v, out), (gvol_rows, gvol_v, gvol)):
        for zz in range(4):
            rows = dot(back, src[zz]).astype(BF)
            mid[:, zz] = rows[:, :128].reshape(32, 8, 128)
            mid[:, zz + 4] = rows[:, 128:].reshape(32, 8, 128)
        store(mid, dst)
    for k in range(27):
        wide = f2[k].astype(F32)
        v2[k] = jnp.concatenate([wide[:, :64], wide[:, 64:]], axis=0)
    store(v2, d2)
    for k in range(27):
        wide = f1[k]
        v1[k] = jnp.concatenate([wide[:, 32 * i : 32 * i + 32] for i in range(4)], axis=0)
    store(v1, d1)
    for i in range(4):
        half, col = i % 2, 128 * (i // 2)
        d4[16 * half : 16 * half + 16, col : col + 128] = f2[27 + i].astype(F32) * scale
    for copy in copies:
        copy.wait()


def halo_scratch(nz, nx, ch):
    return [
        pltpu.VMEM((nz + 2, (nx + 2) * ch, 128), BF),
        pltpu.VMEM((2, 16, nx * ch), BF),
        pltpu.VMEM((3, 2, 3, 16, nx * ch), BF),
    ]


def body(sizes, cells, vol, cot, w1, w2, w3, w4):
    shape = jax.ShapeDtypeStruct
    field = shape((32, 8, 8, 128), BF)
    vmem = pl.BlockSpec(memory_space=pltpu.VMEM)
    nx, ny, nz = sizes
    coarse = 1.0 / math.sqrt(cells / 512.0)
    scales = (1.0 / math.sqrt(cells * 1.0), 1.0 / math.sqrt(cells / 8.0), coarse)
    total = lambda r: [
        pltpu.VMEM((32, r, 128), F32),
        pltpu.VMEM((32, r, 128), F32),
        pltpu.VMEM((nz, r, 128), F32),
        pltpu.VMEM((32, r, 128), F32 if r == 8 else BF),
    ]
    rows = shape((4, 256, 256), BF)
    anywhere = pl.BlockSpec(memory_space=pl.ANY)
    mid = pl.pallas_call(
        functools.partial(kernel, sizes, scales),
        out_shape=[
            rows,
            rows,
            shape((32, 8, 128), F32),
            shape((32, 16, 128), BF),
            shape((ny, 32, 16, 128), BF),
        ],
        in_specs=[pl.BlockSpec(memory_space=pltpu.HBM)] * 6,
        out_specs=[anywhere] * 5,
        scratch_shapes=[
            *halo_scratch(8, 8, 32),
            *halo_scratch(4, 4, 32),
            *halo_scratch(4, 4, 64),
            *halo_scratch(8, 8, 32),
            pltpu.VMEM((6, 960, 256), BF),
            pltpu.VMEM((6, 960, 256), BF),
            pltpu.VMEM((9, 192, 256), BF),
            pltpu.VMEM((9, 384, 256), BF),
            pltpu.VMEM((256, 2880), BF),
            pltpu.VMEM((256, 2880), BF),
            pltpu.VMEM((256, 1728), BF),
            pltpu.VMEM((128, 3456), BF),
            pltpu.VMEM((4, 256, 256), F32),
            pltpu.VMEM((4, 256, 256), BF),
            pltpu.VMEM((4, 256, 256), BF),
            pltpu.VMEM((256, 1024), BF),
            pltpu.VMEM((3, 3, 3, 16, 128), BF),
            pltpu.VMEM((3, 3, 3, 16, 256), BF),
            pltpu.SemaphoreType.DMA((6, 26)),
            pltpu.SemaphoreType.DMA((6, 26)),
            pltpu.VMEM((32, 128), BF),
            pltpu.VMEM(((nz + 2) * (nx + 2), 32, 128), BF),
            pltpu.VMEM((3, (nz + 2) * (nx + 2), 16, 128), BF),
            pltpu.VMEM((8, 8, 256), F32),
            pltpu.VMEM((ny, 8, 256), F32),
            pltpu.VMEM((ny, 32, 16, 128), BF),
            *total(8),
            *total(16),
            pltpu.SemaphoreType.DMA((11,)),
            pltpu.SemaphoreType.DMA((11,)),
            pltpu.VMEM((32, 8, 8, 128), BF),
            pltpu.VMEM((32, 8, 8, 128), BF),
            pltpu.VMEM((27, 32, 32), BF),
            pltpu.VMEM((27, 32, 64), BF),
            pltpu.VMEM((27, 64, 256), BF),
            pltpu.VMEM((32, 256), BF),
            pltpu.VMEM((4, 256, 256), BF),
            pltpu.VMEM((4, 256, 256), BF),
            pltpu.SemaphoreType.DMA((11,)),
        ],
        compiler_params=pltpu.CompilerParams(
            collective_id=0, has_side_effects=True, vmem_limit_bytes=48 * 1024 * 1024
        ),
        name="unet",
    )(vol, cot, w1, jnp.swapaxes(w2, 1, 2), jnp.swapaxes(w3, 1, 2), w4)
    finals = [
        field,
        field,
        shape((27, 32, 32), F32),
        shape((27, 32, 64), F32),
        shape((27, 64, 256), F32),
        shape((32, 256), F32),
    ]
    out, gvol, d1, d2, d3, d4 = pl.pallas_call(
        functools.partial(last_kernel, scales[2] / scales[1]),
        out_shape=finals,
        in_specs=[vmem] * 5,
        out_specs=[anywhere] * 5 + [vmem],
        scratch_shapes=[pltpu.VMEM(f.shape, f.dtype) for f in finals[:5]]
        + [pltpu.SemaphoreType.DMA((5,))],
        compiler_params=pltpu.CompilerParams(vmem_limit_bytes=32 * 1024 * 1024),
        name="finish",
    )(*mid)
    return out, gvol, d1, jnp.swapaxes(d2, 1, 2), jnp.swapaxes(d3, 1, 2), d4


def solution(mesh):
    sizes = (mesh.shape["gx"], mesh.shape["gy"], mesh.shape["gz"])
    cells = 8 * 8 * 128 * sizes[0] * sizes[1] * sizes[2]
    field = P(None, "gz", "gx", "gy")
    return jax.shard_map(
        functools.partial(body, sizes, cells),
        mesh=mesh,
        in_specs=(field, field, P(), P(), P(), P()),
        out_specs=(field, field, P(), P(), P(), P()),
        check_vma=False,
    )
```

profile of v0, /device:TPU:1, one launch (start us, length us, event | category | flops | bytes accessed | tf_op | source)
XLA Modules:
  0.0 83.2 jit_solution(6614838895794650520)
XLA Ops:
  0.6 0.0 copy-start
  0.6 1.2 %copy-done = bf16[27,256,64]{1,2,0:T(8,128)(2,1)S(1)} copy-done((bf16[27,256,64]{1,2,0:T(8,128)(2,1)S(1)}, bf16[27,256,64]{1,2,0:T(8,128)(2,1)}, u32[]{:S(2)}) %copy-start) | copy-done | bytes 884760
  1.8 0.0 copy-start.1
  1.8 1.0 %copy-done.1 = bf16[32,8,8,128]{3,2,1,0:T(8,128)(2,1)S(1)} copy-done((bf16[32,8,8,128]{3,2,1,0:T(8,128)(2,1)S(1)}, bf16[32,8,8,128]{3,2,1,0:T(8,128)(2,1)}, u32[]{:S(2)}) %copy-start.1) | copy-done | bytes 524312
  2.8 0.0 copy-start.2
  2.8 1.0 %copy-done.2 = bf16[32,8,8,128]{3,2,1,0:T(8,128)(2,1)S(1)} copy-done((bf16[32,8,8,128]{3,2,1,0:T(8,128)(2,1)S(1)}, bf16[32,8,8,128]{3,2,1,0:T(8,128)(2,1)}, u32[]{:S(2)}) %copy-start.2) | copy-done | bytes 524312
  3.9 0.0 copy-start.3
  3.9 0.9 %copy-done.3 = bf16[27,32,32]{2,1,0:T(8,128)(2,1)S(1)} copy-done((bf16[27,32,32]{2,1,0:T(8,128)(2,1)S(1)}, bf16[27,32,32]{2,1,0:T(8,128)(2,1)}, u32[]{:S(2)}) %copy-start.3) | copy-done | bytes 55320
  4.8 0.0 copy-start.4
  4.8 0.9 %copy-done.4 = bf16[27,64,32]{1,2,0:T(8,128)(2,1)S(1)} copy-done((bf16[27,64,32]{1,2,0:T(8,128)(2,1)S(1)}, bf16[27,64,32]{1,2,0:T(8,128)(2,1)}, u32[]{:S(2)}) %copy-start.4) | copy-done | bytes 110616
  5.8 0.0 copy-start.5
  5.8 0.7 copy-done.5
  6.5 73.5 %unet.1 = (bf16[4,256,256]{2,1,0:T(8,128)(2,1)S(1)}, bf16[4,256,256]{2,1,0:T(8,128)(2,1)S(1)}, f32[32,8,128]{2,1,0:T(8,128)S(1)}, bf16[32,16,128]{2,1,0:T(8,128)(2,1)S(1)}, bf16[8,32,16,128]{3,2,1,0:T(8,128)(2,1)S(1)}) custom-call(bf16[32,8,8,128]{3,2,1,0:T(8,128)(2,1)S(1)} %copy-done.1, bf16[32,8,8,128]{3,2,1,0:T(8,128)(2,1)S(1)} %copy-done.2, ...), custom_call_target="tpu_custom_call" | custom-call | tf_op jit(solution)/shard_map/unet/pallas_call | solution.py:770
  80.0 3.0 %finish.1 = (bf16[32,8,8,128]{3,2,1,0:T(8,128)(2,1)}, bf16[32,8,8,128]{3,2,1,0:T(8,128)(2,1)}, f32[27,32,32]{2,1,0:T(8,128)}, f32[27,32,64]{2,1,0:T(8,128)}, f32[27,64,256]{2,1,0:T(8,128)}, /*index=5*/f32[32,256]{1,0:T(8,128)}) custom-call(bf16[4,256,256]{2,1,0:T(8,128)(2,1)S(1)} %get-tuple-element.17.out_rows, ...), custom_call_target="tpu_custom_call" | custom-call | tf_op jit(solution)/shard_map/finish/pallas_call | solution.py:835
Async XLA Ops:
  0.6 1.2 %copy-start = (bf16[27,256,64]{1,2,0:T(8,128)(2,1)S(1)}, bf16[27,256,64]{1,2,0:T(8,128)(2,1)}, u32[]{:S(2)}) copy-start(bf16[27,256,64]{1,2,0:T(8,128)(2,1)} %param.10) | copy-start | bytes 2654212
  1.8 1.0 %copy-start.1 = (bf16[32,8,8,128]{3,2,1,0:T(8,128)(2,1)S(1)}, bf16[32,8,8,128]{3,2,1,0:T(8,128)(2,1)}, u32[]{:S(2)}) copy-start(bf16[32,8,8,128]{3,2,1,0:T(8,128)(2,1)} %vol_in.1) | copy-start | bytes 1572868
  2.8 1.0 %copy-start.2 = (bf16[32,8,8,128]{3,2,1,0:T(8,128)(2,1)S(1)}, bf16[32,8,8,128]{3,2,1,0:T(8,128)(2,1)}, u32[]{:S(2)}) copy-start(bf16[32,8,8,128]{3,2,1,0:T(8,128)(2,1)} %cot_in.1) | copy-start | bytes 1572868
  3.9 0.9 %copy-start.3 = (bf16[27,32,32]{2,1,0:T(8,128)(2,1)S(1)}, bf16[27,32,32]{2,1,0:T(8,128)(2,1)}, u32[]{:S(2)}) copy-start(bf16[27,32,32]{2,1,0:T(8,128)(2,1)} %w1_in.1) | copy-start | bytes 165892
  4.8 0.9 %copy-start.4 = (bf16[27,64,32]{1,2,0:T(8,128)(2,1)S(1)}, bf16[27,64,32]{1,2,0:T(8,128)(2,1)}, u32[]{:S(2)}) copy-start(bf16[27,64,32]{1,2,0:T(8,128)(2,1)} %param.9) | copy-start | bytes 331780
  5.8 0.7 copy-start.5
where the time goes:
time: 83.5 us; the launch traced here: 83.2 us
  Pallas kernels  76.5 us (92%)
  local copies, waits for them, and re-layouts  5.83 us (7%)
    pallas_call x1, Pallas kernels, body(): pl.pallas_call(functools.partial(kernel, sizes, scales), out_shape=[rows,...  73.5 us
    unnamed x12, local copies, waits for them, and re-layouts  5.83 us
    pallas_call x1, Pallas kernels, body(): pl.pallas_call(functools.partial(last_kernel, scales[2] / scales[1]), out...  3.04 us

commit v1 on v0

--- a/solution.py
+++ b/solution.py
@@ -238,59 +238,18 @@
             dst[rows * x : rows * (x + 1), base + width * x : base + width * (x + 3)] = band
 
 
-def coarse_start(place, box, send, recv):
-    copies = []
-    for i, (dz, dx, dy) in enumerate(STEPS):
-        copy = pltpu.make_async_remote_copy(
-            src_ref=box.at[1, 1, 1],
-            dst_ref=box.at[1 - dz, 1 - dx, 1 - dy],
-            send_sem=send.at[i],
-            recv_sem=recv.at[i],
-            device_id=place.device(dz, dx, dy),
-            device_id_type=MESH,
-        )
-        copy.start()
-        copies.append(copy)
-    return copies
-
-
-def coarse_shifts(place, box):
-    wide = []
-    for dz, dx in itertools.product((-1, 0, 1), (-1, 0, 1)):
-        rows = []
-        for dy in (-1, 0, 1):
-            block = box[dz + 1, dx + 1, dy + 1]
-            for axis, step in (("z", dz), ("x", dx), ("y", dy)):
-                if step:
-                    block = jnp.where(place.inside(axis, step), block, jnp.zeros_like(block))
-            rows.append(block)
-        wide.append(jnp.concatenate(rows, axis=0))
-    wide = jnp.concatenate(wide, axis=1)
-    r, c = rows_cols((48, 48))
-    pick = hot(c == (r & 15) + (r >> 4) + 15)
-    width = box.shape[-1]
-    return dot(pick, wide).astype(BF), wide[8:40, 4 * width : 5 * width]
-
-
 class Group:
     def __init__(self, place, kind, send, recv):
         self.place, self.kind, self.send, self.recv = place, kind, send, recv
         size = place.size
         self.count = {
-            "plane": size["x"] * size["z"],
             "sheet": size["x"] * size["y"],
-            "line": size["y"],
+            "row": size["x"],
             "depth": size["z"],
-            "chips": size["y"] // 2,
-            "cores": 2,
         }[kind]
 
     def member(self, q):
         at, size = self.place.at, self.place.size
-        if self.kind == "plane":
-            x = lax.rem(at["x"] + q // size["z"], size["x"])
-            z = lax.rem(at["z"] + lax.rem(q, size["z"]), size["z"])
-            return (x, at["y"], z), x * size["z"] + z
         if self.kind == "sheet":
             x = lax.rem(at["x"] + q // size["y"], size["x"])
             y = lax.rem(at["y"] + lax.rem(q, size["y"]), size["y"])
@@ -298,14 +257,8 @@
         if self.kind == "depth":
             z = lax.rem(at["z"] + q, size["z"])
             return (at["x"], at["y"], z), z
-        if self.kind == "line":
-            y = lax.rem(at["y"] + q, size["y"])
-            return (at["x"], y, at["z"]), y
-        if self.kind == "chips":
-            y = lax.rem(at["y"] + 2 * q, size["y"])
-            return (at["x"], y, at["z"]), y // 2
-        y = at["y"] + 1 - 2 * lax.rem(at["y"], 2)
-        return (at["x"], y, at["z"]), lax.rem(y, 2)
+        x = lax.rem(at["x"] + q, size["x"])
+        return (x, at["y"], at["z"]), x
 
     def start(self, src, dst):
         def one(q, carry):
@@ -322,8 +275,7 @@
 
         lax.fori_loop(1, self.count, one, 0)
 
-    def _all(self, slots):
-        ref = slots.at[pl.ds(0, self.count - 1)]
+    def _all(self, ref):
         return pltpu.make_async_remote_copy(
             src_ref=ref,
             dst_ref=ref,
@@ -333,13 +285,15 @@
             device_id_type=MESH,
         )
 
-    def arrive(self, slots):
-        if self.count > 1:
-            self._all(slots).wait_recv()
-
-    def finish(self, slots):
-        if self.count > 1:
-            self._all(slots).wait_send()
+    def arrive(self, ref):
+        self._all(ref).wait_recv()
+
+    def finish(self, ref):
+        self._all(ref).wait_send()
+
+
+def some(ref, count):
+    return ref.at[pl.ds(0, count)]
 
 
 class Total:
@@ -356,25 +310,25 @@
         self.landed[self.me] = self.mine[self.me]
 
     def cross(self):
-        self.one.arrive(self.landed)
+        self.one.arrive(some(self.landed, self.one.count - 1))
         self.line[self.at["z"]] = jnp.sum(self.landed[...], axis=0)
         own = self.line.at[self.at["z"]]
         self.two.start(lambda index: own, own)
 
     def gather(self, scale):
-        self.two.arrive(self.line)
+        self.two.arrive(some(self.line, self.two.count - 1))
         total = jnp.sum(self.line[...], axis=0) * scale
         self.done[self.me] = total.astype(self.done.dtype)
         own = self.done.at[self.me]
         self.three.start(lambda index: own, own)
 
     def arrive(self):
-        self.three.arrive(self.done)
+        self.three.arrive(some(self.done, self.one.count - 1))
 
     def finish(self):
-        self.one.finish(self.landed)
-        self.two.finish(self.line)
-        self.three.finish(self.done)
+        self.one.finish(some(self.landed, self.one.count - 1))
+        self.two.finish(some(self.line, self.two.count - 1))
+        self.three.finish(some(self.done, self.one.count - 1))
 
 
 def kernel(
@@ -383,24 +337,18 @@
     v_pad, v_face, v_got, q_pad, q_face, q_got,
     h_pad, h_face, h_got, g_pad, g_face, g_got,
     u1, ug, u2, uh, t1, tt1, t2, tt2,
-    sl1, act1, cot1, g1, box_in, box_gp, send, recv,
-    note, seen, near_y, tap_sum, tap_line, tap_all,
+    sl1, act1, cot1, g1, send, recv,
+    zbox, note, wide1, wide2, near_y, tap_part, tap_sum, tap_line, tap_all,
     m1, l1, y1, f1, m2, l2, y2, f2, gsend, grecv,
-    vol, cot, w1, w2, w3, w4, out_rows, gvol_rows, local,
+    vol, cot, w1, w2, w3, w4, out_v, gvol_v, local, zsend, zrecv, csend, crecv,
 ):
     place = Place(sizes)
-    seen[...] = jnp.zeros(seen.shape, BF)
     barrier = pltpu.get_barrier_semaphore()
-    partners = [place.device(*s) for s in STEPS if s[0] != 0 and s[2] != 0]
+    partners = [place.device(*s) for s in STEPS if s[0] != 0 and s[1:] != (0, 0)]
     for device in partners:
         pl.semaphore_signal(barrier, inc=1, device_id=device, device_id_type=MESH)
-    sums = [
-        Group(place, kind, gsend.at[i], grecv.at[i])
-        for i, kind in enumerate(("plane", "line", "plane", "chips", "cores"))
-    ]
-    gather, across, plane, chips, cores = sums
     total = len(partners)
-    for kind in ("plane", "sheet"):
+    for kind in ("sheet", "depth"):
         group = Group(place, kind, None, None)
 
         def greet(q, carry, group=group):
@@ -410,6 +358,10 @@
 
         lax.fori_loop(1, group.count, greet, 0)
         total += group.count - 1
+    across, deep, row = [
+        Group(place, kind, gsend.at[i], grecv.at[i])
+        for i, kind in enumerate(("depth", "depth", "row"))
+    ]
     loads = [
         pltpu.make_async_copy(src, dst, local.at[i])
         for i, (src, dst) in enumerate(
@@ -429,12 +381,24 @@
         stores.append(copy)
 
     ix, iy, iz = place.at["x"], place.at["y"], place.at["z"]
-    nx, nz = place.size["x"], place.size["z"]
-    me = ix * nz + iz
+    nx, ny = place.size["x"], place.size["y"]
+    me = ix * ny + iy
+    for wide in (wide1, wide2):
+        for x in range(nx + 4):
+            pads = (0, ny + 1) if 2 <= x < nx + 2 else range(ny + 2)
+            for y in pads:
+                wide[x * (ny + 2) + y] = jnp.zeros((16, 256), BF)
     m1[27:32] = jnp.zeros((5, 8, 128), F32)
     m2[27:32] = jnp.zeros((5, 16, 128), F32)
     r, c = rows_cols((256, 256))
     perm = hot(((r & 31) == (c >> 3)) & ((r >> 5) == (c & 7)))
+    back = hot(((c & 31) == (r >> 3)) & ((c >> 5) == (r & 7)))
+
+    def fine_rows(dst, zz, rows):
+        rows = dot(back, rows).astype(BF)
+        dst[:, zz] = rows[:, :128].reshape(32, 8, 128)
+        dst[:, zz + 4] = rows[:, 128:].reshape(32, 8, 128)
+
 
     def two(ref, zz):
         return jnp.concatenate(
@@ -520,44 +484,109 @@
     own = dot(hot(c == 4 * r), jnp.concatenate([cin, zero], axis=0), NT)
     own += dot(hot(c == 8 * r), jnp.concatenate([zero, cg, zero[:32]], axis=0), NT)
     own = own.astype(BF)
-    box_in[1, 1, 1] = own
-    first = coarse_start(place, box_in, send.at[4], recv.at[4])
-    for copy in first:
+    zbox[2] = own
+    above = []
+    for step in (-2, -1, 1, 2):
+        copy = pltpu.make_async_remote_copy(
+            src_ref=zbox.at[2],
+            dst_ref=zbox.at[2 - step],
+            send_sem=zsend.at[step + 2],
+            recv_sem=zrecv.at[step + 2],
+            device_id=place.device(step, 0, 0),
+            device_id_type=MESH,
+        )
+        copy.start()
+        above.append(copy)
+    for copy in above:
         copy.wait_recv()
-    near, own = coarse_shifts(place, box_in)
-    note[...] = own
-
-    def tap(kz, kx, ky, width, valid):
-        base = (kz * 3 + kx) * width
-        return near[16 * ky : 16 * (ky + 1), base : base + valid]
-
+    zs = []
+    for step in range(-2, 3):
+        block = zbox[step + 2]
+        if step:
+            at = iz + step
+            block = jnp.where((at >= 0) & (at < place.size["z"]), block, jnp.zeros_like(block))
+        zs.append(block)
+    zero = jnp.zeros((16, 64), BF)
+    cin, cg = [z[:, :64] for z in zs], [z[:, 64:96] for z in zs]
+    note[0] = jnp.concatenate([cin[1], cin[2], cin[3], cg[2], zero[:, :32]], axis=1)
+    note[1] = jnp.concatenate([cin[0], cin[4], cg[1], cg[3], zero], axis=1)
+    mine = (ix + 2) * (ny + 2) + iy + 1
+
+    def send_wide(which, dst, kind, dx, dy):
+        pltpu.make_async_remote_copy(
+            src_ref=note.at[which],
+            dst_ref=dst.at[mine],
+            send_sem=zsend.at[kind],
+            recv_sem=zrecv.at[kind],
+            device_id=place.device(0, dx, dy),
+            device_id_type=MESH,
+        ).start()
+
+    def all_wide(dst, kind, count):
+        ref = some(dst, count)
+        return pltpu.make_async_remote_copy(
+            src_ref=ref,
+            dst_ref=ref,
+            send_sem=zsend.at[kind],
+            recv_sem=zrecv.at[kind],
+            device_id=place.device(0, 0, 1),
+            device_id_type=MESH,
+        )
+
+    for dy, dx in itertools.product((-1, 1, 0), range(nx)):
+        if (dy, dx) != (0, 0):
+            send_wide(0, wide1, 5, dx, dy)
+            send_wide(1, wide2, 6, dx, dy)
+
+    far = (ny - 3) * nx
+    wide1[mine] = note[0]
+    wide2[mine] = note[1]
     taps = list(itertools.product(range(3), range(3), range(3)))
-    x3 = jnp.concatenate([tap(*k, 128, 64) for k in taps], axis=1)
-    pre3 = dot(x3, w3[...].reshape(1728, 256))
+
+    def w3_rows(kx, ky):
+        return jnp.concatenate([w3[kz * 9 + kx * 3 + ky] for kz in range(3)], axis=0)
+
+    all_wide(wide1, 5, 3 * nx - 1).wait_recv()
+    all_wide(wide2, 6, 3 * nx - 1).wait_recv()
+
+    def send_far(q, carry):
+        send_wide(0, wide1, 7, lax.rem(q, nx), 2 + q // nx)
+        return carry
+
+    lax.fori_loop(0, far, send_far, 0)
+
+    near, grads = [], []
+    for j in range(5):
+        slots = pl.ds((ix + j) * (ny + 2) + iy, 3)
+        one, two_ = wide1[slots].reshape(48, 256), wide2[slots].reshape(48, 256)
+        near += [two_[:, :64], one[:, :192], two_[:, 64:128]]
+        grads.append([two_[8:40, 128:160], one[8:40, 192:224], two_[8:40, 160:192]])
+    r, c = rows_cols((96, 48))
+    near = dot(hot(c == (r & 31) + (r >> 5) + 7), jnp.concatenate(near, axis=1)).astype(BF)
+    pre3 = 0.0
+    for kx, ky in itertools.product(range(3), range(3)):
+        rows = [
+            near[32 * ky : 32 * ky + 32, 320 * (j + kx) + 64 * z :][:, :192]
+            for z, j in itertools.product(range(3), range(3))
+        ]
+        pre3 = pre3 + dot(jnp.concatenate(rows, axis=0), w3_rows(kx, ky))
     act3, slope3 = silu_slope(pre3)
-    act3 = act3.astype(BF)
-    cgt = own[8:24, 64:96]
-    gp3 = (dot(cgt, w4[...]) * slope3).astype(BF)
-    box_gp[1, 1, 1] = gp3
-    second = coarse_start(place, box_gp, send.at[5], recv.at[5])
-    gather.start(lambda index: note, seen.at[(iz + 1) * (nx + 2) + ix + 1])
-    seen[(iz + 1) * (nx + 2) + ix + 1] = own
-    co = dot(w4[...], act3, NT).astype(BF)
-    part4 = dot(cgt, act3, TN)
-    for i in range(4):
-        half, col = i % 2, 128 * (i // 2)
-        m2[27 + i] = part4[16 * half : 16 * half + 16, col : col + 128]
-    r, c = rows_cols((16, 128))
-    co = dot(co, hot(r == (c >> 3)))
-    co = jnp.concatenate([jnp.concatenate([co] * 8, axis=0)] * 2, axis=1)
-    for zz in range(4):
-        out_rows[zz] = (act1[zz].astype(F32) + co).astype(BF)
-    store(out_rows, out)
-    for copy in second:
-        copy.wait_recv()
-    near = coarse_shifts(place, box_gp)[0]
+    act3 = act3[136:152].astype(BF)
+    cgs = jnp.concatenate(
+        [grads[j + 1][z] for z, j in itertools.product(range(3), range(3))], axis=0
+    )
+    cgt = own[:, 64:96]
+    gp3 = (dot(cgs, w4[...]) * slope3).astype(BF)
+    r, c = rows_cols((48, 32))
+    near = jnp.concatenate([gp3[32 * i : 32 * i + 32] for i in range(9)], axis=1)
+    near = dot(hot(c == (r & 15) + (r >> 4) + 7), near).astype(BF)
+
+    def tap(kz, kx, ky):
+        base = (kz * 3 + kx) * 256
+        return near[16 * ky : 16 * (ky + 1), base : base + 256]
+
     gc = sum(
-        dot(w3[kz * 9 + kx * 3 + ky], tap(2 - kz, 2 - kx, 2 - ky, 256, 256), NT)
+        dot(w3[kz * 9 + kx * 3 + ky], tap(2 - kz, 2 - kx, 2 - ky), NT)
         for kz, kx, ky in taps
     )
     r, c = rows_cols((16, 256))
@@ -566,6 +595,11 @@
     gp2 = (jnp.concatenate([up] * 4, axis=0) * slope2).astype(BF)
     put_half(hh, gp2)
     hh.start()
+    co = dot(w4[...], act3, NT).astype(BF)
+    part4 = dot(cgt, act3, TN)
+    for i in range(4):
+        half, col = i % 2, 128 * (i // 2)
+        m2[27 + i] = part4[16 * half : 16 * half + 16, col : col + 128]
     lane = rows_cols((16, 128))[1]
     for kz in range(3):
         g = dot(u2[3 * kz : 3 * kz + 3].reshape(576, 256), gp2, NT)
@@ -578,44 +612,40 @@
             low = (even + roll(odd, 64))[:16]
             high = (roll(even, 64) + odd)[16:]
             m2[kz * 9 + kx * 3 + ky] = jnp.where(lane < 64, low, high)
-    sum2.scatter()
-    gather.arrive(seen)
-    for ky in range(3):
-        near_y[ky] = seen[:, 7 + ky : 23 + ky, :]
-    lane = rows_cols((16, 128))[1]
-    pair = jnp.where(lane < 64, near_y[0], pltpu.roll(near_y[1], 64, 2))
-    both = jnp.concatenate([pair, near_y[2]], axis=2)
-    both = both.reshape(nz + 2, nx + 2, 16, 256)
-    pre = sum(
-        dot(
-            both[kz : kz + nz, kx : kx + nx].reshape(nz * nx * 16, 256)[:, :192],
-            w3[kz * 9 + kx * 3 : kz * 9 + kx * 3 + 3].reshape(192, 256),
-        )
-        for kz, kx in itertools.product(range(3), range(3))
-    )
+    r, c = rows_cols((16, 128))
+    co = dot(co, hot(r == (c >> 3)))
+    co = jnp.concatenate([jnp.concatenate([co] * 8, axis=0)] * 2, axis=1)
+    for zz in range(4):
+        fine_rows(out_v, zz, (act1[zz].astype(F32) + co).astype(BF))
+    store(out_v, out)
+    all_wide(wide1, 7, far).wait_recv()
+    for x in range(nx + 2):
+        start = (x + 1) * (ny + 2)
+        rows = wide1[start : start + ny + 2].reshape(16 * (ny + 2), 256)
+        for ky in range(3):
+            near_y[ky, x] = rows[15 + ky : 15 + ky + 16 * ny]
+    size = nx * 16 * ny
+    pre = 0.0
+    for kx, ky in itertools.product(range(3), range(3)):
+        rows = near_y[ky, kx : kx + nx].reshape(size, 256)[:, :192]
+        pre = pre + dot(rows, w3_rows(kx, ky))
     slope = silu_slope(pre)[1]
-    mid = near_y[1].reshape(nz + 2, nx + 2, 16, 128)[1 : nz + 1, 1 : nx + 1]
-    mid = mid.reshape(nz * nx * 16, 128)[:, 64:96]
-    gp = (dot(mid, w4[...]) * slope).astype(BF)
+    cgs = near_y[1, 1 : nx + 1].reshape(size, 256)[:, 192:224]
+    gp = (dot(cgs, w4[...]) * slope).astype(BF)
     k = lax.rem(me, 27)
     kz, kx, ky = k // 9, lax.rem(k // 3, 3), lax.rem(k, 3)
-    rows = jnp.concatenate(
-        [
-            near_y[ky, pl.ds((z + kz) * (nx + 2) + kx, nx)].reshape(nx * 16, 128)
-            for z in range(nz)
-        ],
-        axis=0,
-    )
-    tap_sum[...] = dot(rows, gp, TN)[:64].reshape(8, 8, 256)
-    across.start(lambda index: tap_sum.at[index], tap_line.at[iy])
-    tap_line[iy] = tap_sum[iy]
+    rows = near_y[ky, pl.ds(kx, nx)].reshape(size, 256)
+    tap_part[...] = dot(rows, gp, TN).reshape(4, 8, 8, 256)
+    tap_sum[...] = tap_part[kz]
+    across.start(lambda index: tap_sum.at[index], tap_line.at[iz])
+    tap_line[iz] = tap_sum[iz]
     hh.arrive()
-    across.arrive(tap_line)
+    sum2.scatter()
+    across.arrive(some(tap_line, across.count - 1))
     s = jnp.sum(tap_line[...], axis=0) * scales[2]
-    tap_all[iy, me] = jnp.concatenate([s[:, :128], s[:, 128:]], axis=0).astype(BF)
-    own_tap = tap_all.at[iy, me]
-    plane.start(lambda index: own_tap, own_tap)
-    sum2.cross()
+    tap_all[ix, iy, iz] = jnp.concatenate([s[:, :128], s[:, 128:]], axis=0).astype(BF)
+    own_tap = tap_all.at[ix, iy, iz]
+    deep.start(lambda index: own_tap, own_tap)
     fill_half(hh, uh)
     gpool = dot(tt2[...], uh[...].reshape(3456, 256))
     r, c = rows_cols((256, 256))
@@ -646,58 +676,64 @@
                 )
     sum1.scatter()
     hg.start()
-    plane.arrive(tap_all.at[iy])
-    own_range = tap_all.at[iy]
-    chips.start(lambda index: own_range, own_range)
+    deep_all = some(tap_all.at[ix, iy], deep.count - 1)
+    deep.arrive(deep_all)
+    own_depth = tap_all.at[ix, iy]
+    row.start(lambda index: own_depth, own_depth)
+    sum2.cross()
     sum1.cross()
-    sum2.gather(scales[1])
+    row_all = tap_all.at[pl.ds(0, nx - 1), iy]
+    row.arrive(row_all)
+    other = iy + 1 - 2 * lax.rem(iy, 2)
+
+    def range_copy(y, target, lane):
+        block = tap_all.at[pl.ds(0, nx), y]
+        return pltpu.make_async_remote_copy(
+            src_ref=block,
+            dst_ref=block,
+            send_sem=csend.at[lane],
+            recv_sem=crecv.at[lane],
+            device_id=(ix, target, iz),
+            device_id_type=MESH,
+        )
+
+    hops = range(1, ny // 2)
+    ranges = [range_copy(iy, lax.rem(iy + 2 * s, ny), s) for s in hops]
+    for copy in ranges:
+        copy.start()
+    passed = [range_copy(iy, other, ny // 2)]
+    passed[0].start()
     hg.arrive()
     fill_fine(hg, ug)
+    sum2.gather(scales[1])
     sum1.gather(scales[0])
     for zz in range(4):
         rows = dot(tt1[...], ug[zz : zz + 3].reshape(2880, 256))
-        gvol_rows[zz] = rows.astype(BF)
-    store(gvol_rows, gvol)
-    chips.arrive(tap_all)
-    core = lax.rem(iy, 2)
-
-    def to_core(c, carry):
-        own = tap_all.at[2 * c + core]
-        pltpu.make_async_remote_copy(
-            src_ref=own,
-            dst_ref=own,
-            send_sem=cores.send,
-            recv_sem=cores.recv,
-            device_id=cores.member(1)[0],
-            device_id_type=MESH,
-        ).start()
-        return carry
-
-    lax.fori_loop(0, chips.count, to_core, 0)
+        fine_rows(gvol_v, zz, rows.astype(BF))
+    store(gvol_v, gvol)
+    for s, copy in zip(hops, ranges):
+        copy.wait_recv()
+        passed.append(range_copy(lax.rem(iy + ny - 2 * s, ny), other, ny // 2 + s))
+        passed[-1].start()
     sum2.arrive()
     store(f2, d2)
     sum1.arrive()
     store(f1, d1)
-    rest = tap_all.at[pl.ds(0, chips.count)]
-    rest = pltpu.make_async_remote_copy(
-        src_ref=rest,
-        dst_ref=rest,
-        send_sem=cores.send,
-        recv_sem=cores.recv,
-        device_id=cores.member(1)[0],
-        device_id_type=MESH,
-    )
-    rest.wait_recv()
+    for copy in passed:
+        copy.wait_recv()
     store(tap_all, d3)
-    rest.wait_send()
+    for copy in ranges + passed:
+        copy.wait_send()
     for halo in (hv, hq, hh, hg):
         halo.finish()
-    for copy in first + second:
+    for copy in above:
         copy.wait_send()
-    gather.finish(seen)
-    across.finish(tap_line)
-    plane.finish(tap_all.at[iy])
-    chips.finish(tap_all)
+    all_wide(wide1, 5, 3 * nx - 1).wait_send()
+    all_wide(wide2, 6, 3 * nx - 1).wait_send()
+    all_wide(wide1, 7, far).wait_send()
+    across.finish(some(tap_line, across.count - 1))
+    deep.finish(deep_all)
+    row.finish(row_all)
     sum1.finish()
     sum2.finish()
     for copy in stores:
@@ -705,43 +741,49 @@
 
 
 def last_kernel(
-    scale, out_rows, gvol_rows, f1, f2, tap_all,
+    scale, out_in, gvol_in, f1_in, f2_in, tap_in,
     out, gvol, d1, d2, d3, d4,
-    out_v, gvol_v, v1, v2, v3, sems,
+    f1, f2, tap_all, out_v, gvol_v, v1, v2, v3, sems,
 ):
-    r, c = rows_cols((256, 256))
-    back = hot(((c & 31) == (r >> 3)) & ((c >> 5) == (r & 7)))
     copies = []
 
-    def store(src, dst):
-        copy = pltpu.make_async_copy(src, dst, sems.at[len(copies)])
-        copy.start()
-        copies.append(copy)
-
-    for j in range(tap_all.shape[0]):
-        for k in range(27):
-            block = tap_all[j, k].astype(F32)
+    def copy(src, dst):
+        one = pltpu.make_async_copy(src, dst, sems.at[len(copies)])
+        one.start()
+        copies.append(one)
+        return one
+
+    loads = [
+        copy(tap_in, tap_all), copy(f2_in, f2), copy(f1_in, f1),
+        copy(out_in, out_v), copy(gvol_in, gvol_v),
+    ]
+    loads[0].wait()
+    for k in range(27):
+        for j in range(8):
+            block = tap_all[k // 8, k % 8, j].astype(F32)
             v3[k, 8 * j : 8 * j + 8, :] = jnp.concatenate([block[:8], block[8:]], axis=1)
-    store(v3, d3)
-    for src, mid, dst in ((out_rows, out_v, out), (gvol_rows, gvol_v, gvol)):
-        for zz in range(4):
-            rows = dot(back, src[zz]).astype(BF)
-            mid[:, zz] = rows[:, :128].reshape(32, 8, 128)
-            mid[:, zz + 4] = rows[:, 128:].reshape(32, 8, 128)
-        store(mid, dst)
+        if k % 9 == 8:
+            copy(v3.at[pl.ds(k - 8, 9)], d3.at[pl.ds(k - 8, 9)])
+        if k == 8:
+            for load in loads[3:]:
+                load.wait()
+            copy(out_v, out)
+            copy(gvol_v, gvol)
+    loads[1].wait()
     for k in range(27):
         wide = f2[k].astype(F32)
         v2[k] = jnp.concatenate([wide[:, :64], wide[:, 64:]], axis=0)
-    store(v2, d2)
+    copy(v2, d2)
+    loads[2].wait()
     for k in range(27):
         wide = f1[k]
         v1[k] = jnp.concatenate([wide[:, 32 * i : 32 * i + 32] for i in range(4)], axis=0)
-    store(v1, d1)
+    copy(v1, d1)
     for i in range(4):
         half, col = i % 2, 128 * (i // 2)
         d4[16 * half : 16 * half + 16, col : col + 128] = f2[27 + i].astype(F32) * scale
-    for copy in copies:
-        copy.wait()
+    for one in copies[5:]:
+        one.wait()
 
 
 def halo_scratch(nz, nx, ch):
@@ -765,18 +807,17 @@
         pltpu.VMEM((nz, r, 128), F32),
         pltpu.VMEM((32, r, 128), F32 if r == 8 else BF),
     ]
-    rows = shape((4, 256, 256), BF)
     anywhere = pl.BlockSpec(memory_space=pl.ANY)
     mid = pl.pallas_call(
         functools.partial(kernel, sizes, scales),
         out_shape=[
-            rows,
-            rows,
+            field,
+            field,
             shape((32, 8, 128), F32),
             shape((32, 16, 128), BF),
-            shape((ny, 32, 16, 128), BF),
+            shape((nx, ny, 8, 16, 128), BF),
         ],
-        in_specs=[pl.BlockSpec(memory_space=pltpu.HBM)] * 6,
+        in_specs=[anywhere] * 6,
         out_specs=[anywhere] * 5,
         scratch_shapes=[
             *halo_scratch(8, 8, 32),
@@ -795,16 +836,17 @@
             pltpu.VMEM((4, 256, 256), BF),
             pltpu.VMEM((4, 256, 256), BF),
             pltpu.VMEM((256, 1024), BF),
-            pltpu.VMEM((3, 3, 3, 16, 128), BF),
-            pltpu.VMEM((3, 3, 3, 16, 256), BF),
-            pltpu.SemaphoreType.DMA((6, 26)),
-            pltpu.SemaphoreType.DMA((6, 26)),
-            pltpu.VMEM((32, 128), BF),
-            pltpu.VMEM(((nz + 2) * (nx + 2), 32, 128), BF),
-            pltpu.VMEM((3, (nz + 2) * (nx + 2), 16, 128), BF),
+            pltpu.SemaphoreType.DMA((4, 26)),
+            pltpu.SemaphoreType.DMA((4, 26)),
+            pltpu.VMEM((5, 16, 128), BF),
+            pltpu.VMEM((2, 16, 256), BF),
+            pltpu.VMEM(((nx + 4) * (ny + 2), 16, 256), BF),
+            pltpu.VMEM(((nx + 4) * (ny + 2), 16, 256), BF),
+            pltpu.VMEM((3, nx + 2, 16 * ny, 256), BF),
+            pltpu.VMEM((4, 8, 8, 256), F32),
             pltpu.VMEM((8, 8, 256), F32),
-            pltpu.VMEM((ny, 8, 256), F32),
-            pltpu.VMEM((ny, 32, 16, 128), BF),
+            pltpu.VMEM((nz, 8, 256), F32),
+            pltpu.VMEM((nx, ny, 8, 16, 128), BF),
             *total(8),
             *total(16),
             pltpu.SemaphoreType.DMA((11,)),
@@ -815,12 +857,16 @@
             pltpu.VMEM((27, 32, 64), BF),
             pltpu.VMEM((27, 64, 256), BF),
             pltpu.VMEM((32, 256), BF),
-            pltpu.VMEM((4, 256, 256), BF),
-            pltpu.VMEM((4, 256, 256), BF),
+            pltpu.VMEM((32, 8, 8, 128), BF),
+            pltpu.VMEM((32, 8, 8, 128), BF),
             pltpu.SemaphoreType.DMA((11,)),
+            pltpu.SemaphoreType.DMA((8,)),
+            pltpu.SemaphoreType.DMA((8,)),
+            pltpu.SemaphoreType.DMA((ny,)),
+            pltpu.SemaphoreType.DMA((ny,)),
         ],
         compiler_params=pltpu.CompilerParams(
-            collective_id=0, has_side_effects=True, vmem_limit_bytes=48 * 1024 * 1024
+            collective_id=0, has_side_effects=True, vmem_limit_bytes=60 * 1024 * 1024
         ),
         name="unet",
     )(vol, cot, w1, jnp.swapaxes(w2, 1, 2), jnp.swapaxes(w3, 1, 2), w4)
@@ -835,11 +881,11 @@
     out, gvol, d1, d2, d3, d4 = pl.pallas_call(
         functools.partial(last_kernel, scales[2] / scales[1]),
         out_shape=finals,
-        in_specs=[vmem] * 5,
+        in_specs=[anywhere] * 5,
         out_specs=[anywhere] * 5 + [vmem],
-        scratch_shapes=[pltpu.VMEM(f.shape, f.dtype) for f in finals[:5]]
-        + [pltpu.SemaphoreType.DMA((5,))],
-        compiler_params=pltpu.CompilerParams(vmem_limit_bytes=32 * 1024 * 1024),
+        scratch_shapes=[pltpu.VMEM(f.shape, f.dtype) for f in list(mid[2:]) + finals[:5]]
+        + [pltpu.SemaphoreType.DMA((12,))],
+        compiler_params=pltpu.CompilerParams(vmem_limit_bytes=60 * 1024 * 1024),
         name="finish",
     )(*mid)
     return out, gvol, d1, jnp.swapaxes(d2, 1, 2), jnp.swapaxes(d3, 1, 2), d4

time: 83.5 us -> 77.6 us (0.929)
  local copies, waits for them, and re-layouts: 5.83 us -> 0 us
    unnamed x12 -> x0, local copies, waits for them, and re-layouts: 5.83 us -> none
    pallas_call x1, Pallas kernels: 3.04 us -> 3.95 us  [body(): pl.pallas_call(functools.partial(last_kernel, scales[2] / scales[1]), out...]
where the time goes in v1:
time: 77.6 us; the launch traced here: 77.5 us
  Pallas kernels  76.7 us (99%)
  between operations  0.8 us (1%)
    pallas_call x1, Pallas kernels, body(): pl.pallas_call(functools.partial(kernel, sizes, scales), out_shape=[field...  72.7 us
    pallas_call x1, Pallas kernels, body(): pl.pallas_call(functools.partial(last_kernel, scales[2] / scales[1]), out...  3.95 us

profile of v1, /device:TPU:1, one launch (start us, length us, event | category | flops | bytes accessed | tf_op | source)
XLA Modules:
  0.0 77.5 jit_solution(16393861418038959321)
XLA Ops:
  0.6 72.7 %unet.1 = (bf16[32,8,8,128]{3,2,1,0:T(8,128)(2,1)}, bf16[32,8,8,128]{3,2,1,0:T(8,128)(2,1)}, f32[32,8,128]{2,1,0:T(8,128)}, bf16[32,16,128]{2,1,0:T(8,128)(2,1)}, bf16[4,8,8,16,128]{4,3,2,1,0:T(8,128)(2,1)}) custom-call(bf16[32,8,8,128]{3,2,1,0:T(8,128)(2,1)} %vol_in.1, bf16[32,8,8,128]{3,2,1,0:T(8,128)(2,1)} %cot_in.1, bf16[27,32,32]{2,1,0:T(8,128)(2,1)} %w1_in.1, ...), custom_call_target="tpu_custom_call" | custom-call | tf_op jit(solution)/shard_map/unet/pallas_call | solution.py:811
  73.4 4.0 %finish.1 = (bf16[32,8,8,128]{3,2,1,0:T(8,128)(2,1)}, bf16[32,8,8,128]{3,2,1,0:T(8,128)(2,1)}, f32[27,32,32]{2,1,0:T(8,128)}, f32[27,32,64]{2,1,0:T(8,128)}, f32[27,64,256]{2,1,0:T(8,128)}, /*index=5*/f32[32,256]{1,0:T(8,128)}) custom-call(bf16[32,8,8,128]{3,2,1,0:T(8,128)(2,1)} %get-tuple-element.17.out_in, ...), custom_call_target="tpu_custom_call" | custom-call | tf_op jit(solution)/shard_map/finish/pallas_call | solution.py:881

commit v2 on v1

--- a/solution.py
+++ b/solution.py
@@ -311,7 +311,7 @@
 
     def cross(self):
         self.one.arrive(some(self.landed, self.one.count - 1))
-        self.line[self.at["z"]] = jnp.sum(self.landed[...], axis=0)
+        self.line[self.at["z"]] = jnp.sum(self.landed[...].astype(F32), axis=0)
         own = self.line.at[self.at["z"]]
         self.two.start(lambda index: own, own)
 
@@ -338,7 +338,7 @@
     h_pad, h_face, h_got, g_pad, g_face, g_got,
     u1, ug, u2, uh, t1, tt1, t2, tt2,
     sl1, act1, cot1, g1, send, recv,
-    zbox, note, wide1, wide2, near_y, tap_part, tap_sum, tap_line, tap_all,
+    zbox, note, wide, near_y, tap_part, tap_sum, tap_line, tap_all,
     m1, l1, y1, f1, m2, l2, y2, f2, gsend, grecv,
     vol, cot, w1, w2, w3, w4, out_v, gvol_v, local, zsend, zrecv, csend, crecv,
 ):
@@ -383,13 +383,12 @@
     ix, iy, iz = place.at["x"], place.at["y"], place.at["z"]
     nx, ny = place.size["x"], place.size["y"]
     me = ix * ny + iy
-    for wide in (wide1, wide2):
-        for x in range(nx + 4):
-            pads = (0, ny + 1) if 2 <= x < nx + 2 else range(ny + 2)
-            for y in pads:
-                wide[x * (ny + 2) + y] = jnp.zeros((16, 256), BF)
+    for x in range(nx + 4):
+        pads = (0, ny + 1) if 2 <= x < nx + 2 else range(ny + 2)
+        for y in pads:
+            wide[x * (ny + 2) + y] = jnp.zeros((16, 512), BF)
     m1[27:32] = jnp.zeros((5, 8, 128), F32)
-    m2[27:32] = jnp.zeros((5, 16, 128), F32)
+    m2[27:32] = jnp.zeros((5, 16, 128), BF)
     r, c = rows_cols((256, 256))
     perm = hot(((r & 31) == (c >> 3)) & ((r >> 5) == (c & 7)))
     back = hot(((c & 31) == (r >> 3)) & ((c >> 5) == (r & 7)))
@@ -508,22 +507,22 @@
         zs.append(block)
     zero = jnp.zeros((16, 64), BF)
     cin, cg = [z[:, :64] for z in zs], [z[:, 64:96] for z in zs]
-    note[0] = jnp.concatenate([cin[1], cin[2], cin[3], cg[2], zero[:, :32]], axis=1)
-    note[1] = jnp.concatenate([cin[0], cin[4], cg[1], cg[3], zero], axis=1)
+    note[:, 0:256] = jnp.concatenate([*cin[1:4], cg[2], zero[:, :32]], axis=1)
+    note[:, 256:512] = jnp.concatenate([cin[0], cin[4], cg[1], cg[3], zero], axis=1)
     mine = (ix + 2) * (ny + 2) + iy + 1
 
-    def send_wide(which, dst, kind, dx, dy):
+    def send_wide(lanes, kind, dx, dy):
         pltpu.make_async_remote_copy(
-            src_ref=note.at[which],
-            dst_ref=dst.at[mine],
+            src_ref=note.at[:, pl.ds(0, lanes)],
+            dst_ref=wide.at[mine, :, pl.ds(0, lanes)],
             send_sem=zsend.at[kind],
             recv_sem=zrecv.at[kind],
             device_id=place.device(0, dx, dy),
             device_id_type=MESH,
         ).start()
 
-    def all_wide(dst, kind, count):
-        ref = some(dst, count)
+    def all_wide(lanes, kind, count):
+        ref = wide.at[pl.ds(0, count), :, pl.ds(0, lanes)]
         return pltpu.make_async_remote_copy(
             src_ref=ref,
             dst_ref=ref,
@@ -535,22 +534,19 @@
 
     for dy, dx in itertools.product((-1, 1, 0), range(nx)):
         if (dy, dx) != (0, 0):
-            send_wide(0, wide1, 5, dx, dy)
-            send_wide(1, wide2, 6, dx, dy)
-
+            send_wide(512, 5, dx, dy)
     far = (ny - 3) * nx
-    wide1[mine] = note[0]
-    wide2[mine] = note[1]
+    wide[mine] = note[...]
     taps = list(itertools.product(range(3), range(3), range(3)))
 
     def w3_rows(kx, ky):
         return jnp.concatenate([w3[kz * 9 + kx * 3 + ky] for kz in range(3)], axis=0)
 
-    all_wide(wide1, 5, 3 * nx - 1).wait_recv()
-    all_wide(wide2, 6, 3 * nx - 1).wait_recv()
+    near_all, far_all = all_wide(512, 5, 3 * nx - 1), all_wide(256, 7, far)
+    near_all.wait_recv()
 
     def send_far(q, carry):
-        send_wide(0, wide1, 7, lax.rem(q, nx), 2 + q // nx)
+        send_wide(256, 7, lax.rem(q, nx), 2 + q // nx)
         return carry
 
     lax.fori_loop(0, far, send_far, 0)
@@ -558,7 +554,8 @@
     near, grads = [], []
     for j in range(5):
         slots = pl.ds((ix + j) * (ny + 2) + iy, 3)
-        one, two_ = wide1[slots].reshape(48, 256), wide2[slots].reshape(48, 256)
+        both = wide[slots].reshape(48, 512)
+        one, two_ = both[:, :256], both[:, 256:]
         near += [two_[:, :64], one[:, :192], two_[:, 64:128]]
         grads.append([two_[8:40, 128:160], one[8:40, 192:224], two_[8:40, 160:192]])
     r, c = rows_cols((96, 48))
@@ -599,7 +596,7 @@
     part4 = dot(cgt, act3, TN)
     for i in range(4):
         half, col = i % 2, 128 * (i // 2)
-        m2[27 + i] = part4[16 * half : 16 * half + 16, col : col + 128]
+        m2[27 + i] = part4[16 * half : 16 * half + 16, col : col + 128].astype(BF)
     lane = rows_cols((16, 128))[1]
     for kz in range(3):
         g = dot(u2[3 * kz : 3 * kz + 3].reshape(576, 256), gp2, NT)
@@ -611,17 +608,12 @@
             even, odd = cut[0] + cut[2], cut[1] + cut[3]
             low = (even + roll(odd, 64))[:16]
             high = (roll(even, 64) + odd)[16:]
-            m2[kz * 9 + kx * 3 + ky] = jnp.where(lane < 64, low, high)
-    r, c = rows_cols((16, 128))
-    co = dot(co, hot(r == (c >> 3)))
-    co = jnp.concatenate([jnp.concatenate([co] * 8, axis=0)] * 2, axis=1)
-    for zz in range(4):
-        fine_rows(out_v, zz, (act1[zz].astype(F32) + co).astype(BF))
-    store(out_v, out)
-    all_wide(wide1, 7, far).wait_recv()
+            m2[kz * 9 + kx * 3 + ky] = jnp.where(lane < 64, low, high).astype(BF)
+    sum2.scatter()
+    far_all.wait_recv()
     for x in range(nx + 2):
         start = (x + 1) * (ny + 2)
-        rows = wide1[start : start + ny + 2].reshape(16 * (ny + 2), 256)
+        rows = wide[start : start + ny + 2, :, 0:256].reshape(16 * (ny + 2), 256)
         for ky in range(3):
             near_y[ky, x] = rows[15 + ky : 15 + ky + 16 * ny]
     size = nx * 16 * ny
@@ -640,7 +632,6 @@
     across.start(lambda index: tap_sum.at[index], tap_line.at[iz])
     tap_line[iz] = tap_sum[iz]
     hh.arrive()
-    sum2.scatter()
     across.arrive(some(tap_line, across.count - 1))
     s = jnp.sum(tap_line[...], axis=0) * scales[2]
     tap_all[ix, iy, iz] = jnp.concatenate([s[:, :128], s[:, 128:]], axis=0).astype(BF)
@@ -676,6 +667,12 @@
                 )
     sum1.scatter()
     hg.start()
+    r, c = rows_cols((16, 128))
+    co = dot(co, hot(r == (c >> 3)))
+    co = jnp.concatenate([jnp.concatenate([co] * 8, axis=0)] * 2, axis=1)
+    for zz in range(4):
+        fine_rows(out_v, zz, (act1[zz].astype(F32) + co).astype(BF))
+    store(out_v, out)
     deep_all = some(tap_all.at[ix, iy], deep.count - 1)
     deep.arrive(deep_all)
     own_depth = tap_all.at[ix, iy]
@@ -728,9 +725,8 @@
         halo.finish()
     for copy in above:
         copy.wait_send()
-    all_wide(wide1, 5, 3 * nx - 1).wait_send()
-    all_wide(wide2, 6, 3 * nx - 1).wait_send()
-    all_wide(wide1, 7, far).wait_send()
+    near_all.wait_send()
+    far_all.wait_send()
     across.finish(some(tap_line, across.count - 1))
     deep.finish(deep_all)
     row.finish(row_all)
@@ -802,8 +798,8 @@
     coarse = 1.0 / math.sqrt(cells / 512.0)
     scales = (1.0 / math.sqrt(cells * 1.0), 1.0 / math.sqrt(cells / 8.0), coarse)
     total = lambda r: [
-        pltpu.VMEM((32, r, 128), F32),
-        pltpu.VMEM((32, r, 128), F32),
+        pltpu.VMEM((32, r, 128), F32 if r == 8 else BF),
+        pltpu.VMEM((32, r, 128), F32 if r == 8 else BF),
         pltpu.VMEM((nz, r, 128), F32),
         pltpu.VMEM((32, r, 128), F32 if r == 8 else BF),
     ]
@@ -839,9 +835,8 @@
             pltpu.SemaphoreType.DMA((4, 26)),
             pltpu.SemaphoreType.DMA((4, 26)),
             pltpu.VMEM((5, 16, 128), BF),
-            pltpu.VMEM((2, 16, 256), BF),
-            pltpu.VMEM(((nx + 4) * (ny + 2), 16, 256), BF),
-            pltpu.VMEM(((nx + 4) * (ny + 2), 16, 256), BF),
+            pltpu.VMEM((16, 512), BF),
+            pltpu.VMEM(((nx + 4) * (ny + 2), 16, 512), BF),
             pltpu.VMEM((3, nx + 2, 16 * ny, 256), BF),
             pltpu.VMEM((4, 8, 8, 256), F32),
             pltpu.VMEM((8, 8, 256), F32),

time: 77.6 us -> 77.8 us (level)
  no operation moved by 1% of the time
where the time goes in v2:
time: 77.8 us; the launch traced here: 77.6 us
  Pallas kernels  76.8 us (99%)
  between operations  0.8 us (1%)
    pallas_call x1, Pallas kernels, body(): pl.pallas_call(functools.partial(kernel, sizes, scales), out_shape=[field...  72.9 us
    pallas_call x1, Pallas kernels, body(): pl.pallas_call(functools.partial(last_kernel, scales[2] / scales[1]), out...  3.95 us

profile of v2, /device:TPU:1, one launch (start us, length us, event | category | flops | bytes accessed | tf_op | source)
XLA Modules:
  0.0 77.6 jit_solution(12020151787497490378)
XLA Ops:
  0.6 72.9 %unet.1 = (bf16[32,8,8,128]{3,2,1,0:T(8,128)(2,1)}, bf16[32,8,8,128]{3,2,1,0:T(8,128)(2,1)}, f32[32,8,128]{2,1,0:T(8,128)}, bf16[32,16,128]{2,1,0:T(8,128)(2,1)}, bf16[4,8,8,16,128]{4,3,2,1,0:T(8,128)(2,1)}) custom-call(bf16[32,8,8,128]{3,2,1,0:T(8,128)(2,1)} %vol_in.1, bf16[32,8,8,128]{3,2,1,0:T(8,128)(2,1)} %cot_in.1, bf16[27,32,32]{2,1,0:T(8,128)(2,1)} %w1_in.1, ...), custom_call_target="tpu_custom_call" | custom-call | tf_op jit(solution)/shard_map/unet/pallas_call | solution.py:807
  73.5 4.0 %finish.1 = (bf16[32,8,8,128]{3,2,1,0:T(8,128)(2,1)}, bf16[32,8,8,128]{3,2,1,0:T(8,128)(2,1)}, f32[27,32,32]{2,1,0:T(8,128)}, f32[27,32,64]{2,1,0:T(8,128)}, f32[27,64,256]{2,1,0:T(8,128)}, /*index=5*/f32[32,256]{1,0:T(8,128)}) custom-call(bf16[32,8,8,128]{3,2,1,0:T(8,128)(2,1)} %get-tuple-element.17.out_in, ...), custom_call_target="tpu_custom_call" | custom-call | tf_op jit(solution)/shard_map/finish/pallas_call | solution.py:876
